TPU v7x, 32 devices: a whole 2x2x4 slice. The times are simulated.
32 devices in a mesh: group: 4 (over z), member: 8 (over y, x, core).
Axes of the slice: x: 2, y: 2, z: 4, core: 2. Of those that a mesh axis runs over, the one named last changes fastest.
Arguments:
- embeddings: bfloat16 [16384, 768], P(('group', 'member')), may hold values from -120 to 120
- cluster_ids: int32 [16384], P(('group', 'member')), may hold values from 0 to 63, as said below
- ranks: int32 [16384], P(('group', 'member')), may hold values from 0 to 16383, each once
Outputs:
- best_similarity: float32 [16384], P(('group', 'member'))
Inputs may be any that keep to these rules, and one draw needn't show every extreme that they name: `cluster_ids`: among the 512 rows of any one device, one residue of the cluster ids modulo 4 has exactly 256 rows, the next residue (modulo 4) none, and every other residue 512 // 4; which residue has 256 depends only on the device's member index, so every residue has exactly 4096 rows in all. The 16 clusters of one residue hold, in some order, (l+1)**2 * 4096 // 16**2 - l**2 * 4096 // 16**2 rows for l = 0 to 15; the largest holds 496.
All inputs are finite; a program needn't handle non-finite values.
Results may differ from a plain program's by a relative error of at most 0.00058.
Values may be sent and summed in bfloat16 or wider, within the bound.
A program may use at most 128 MiB of HBM per device.

v0:
```python
import math

import jax
import jax.numpy as jnp
from jax import lax
from jax.sharding import PartitionSpec as P


def unit_rows(values):
    widened = values.astype(jnp.float32)
    square = jnp.mean(widened * widened, axis=-1, keepdims=True)
    return (widened * lax.rsqrt(square + 1e-06) * (1.0 / math.sqrt(values.shape[-1]))).astype(
        jnp.bfloat16
    )


def best_against(query_side, key_side):
    query_units, query_ids, query_ranks = query_side
    key_units, key_ids, key_ranks = key_side
    query_count = query_units.shape[0]
    key_count = key_units.shape[0]
    key_block = key_count
    while key_block * query_count > 4194304 and key_block % 2 == 0 and (key_block // 2 % 128 == 0):
        key_block = key_block // 2
    shaped = (
        query_units.reshape(query_count // query_count, query_count, query_units.shape[1]),
        query_ids.reshape(query_count // query_count, query_count),
        query_ranks.reshape(query_count // query_count, query_count),
    )
    block_units = shaped[0][0]
    block_ids = shaped[1][0]
    block_ranks = shaped[2][0]

    def advance(position, running):
        offset = position * key_block
        panel_units = lax.dynamic_slice_in_dim(key_units, offset, key_block, 0)
        panel_ids = lax.dynamic_slice_in_dim(key_ids, offset, key_block, 0)
        panel_ranks = lax.dynamic_slice_in_dim(key_ranks, offset, key_block, 0)
        scores = lax.dot_general(
            block_units, panel_units, (((1,), (1,)), ((), ())), preferred_element_type=jnp.float32
        )
        allowed = (
            (block_ids[:, None] == panel_ids[None, :])
            & (panel_ranks[None, :] < block_ranks[:, None])
            & (panel_ids[None, :] >= 0)
        )
        return jnp.maximum(running, jnp.max(jnp.where(allowed, scores, -1.0), axis=1))

    start = jnp.full((query_count,), -1.0, jnp.float32)
    turns = key_count // key_block
    return lax.fori_loop(0, turns, advance, start)


def body(embeddings, cluster_ids, ranks):
    local_rows, features = embeddings.shape
    groups = lax.axis_size("group")
    capacity = 2 * local_rows // groups
    target = cluster_ids % groups
    lane_ids = jnp.arange(groups, dtype=jnp.int32)
    lane_hits = (target[:, None] == lane_ids[None, :]).astype(jnp.int32)
    before = jnp.sum((jnp.cumsum(lane_hits, axis=0) - lane_hits) * lane_hits, axis=1)
    places = target * capacity + before
    slot_count = groups * capacity
    send_rows = jnp.zeros((slot_count, features), jnp.bfloat16).at[places].set(embeddings)
    send_ids = jnp.full((slot_count,), -1, jnp.int32).at[places].set(cluster_ids)
    send_ranks = jnp.zeros((slot_count,), jnp.int32).at[places].set(ranks)
    held_rows, held_ids, held_ranks = (
        lax.all_to_all(send_rows, "group", split_axis=0, concat_axis=0, tiled=True),
        lax.all_to_all(send_ids, "group", split_axis=0, concat_axis=0, tiled=True),
        lax.all_to_all(send_ranks, "group", split_axis=0, concat_axis=0, tiled=True),
    )
    held_units = unit_rows(held_rows)
    resident_count = held_ids.shape[0]
    best_score = jnp.maximum(
        jnp.full((resident_count,), -1.0, jnp.float32),
        best_against(
            (held_units, held_ids, held_ranks),
            (
                lax.all_gather(held_units, "member", axis=0, tiled=True),
                lax.all_gather(held_ids, "member", axis=0, tiled=True),
                lax.all_gather(held_ranks, "member", axis=0, tiled=True),
            ),
        ),
    )
    returned = lax.all_to_all(best_score, "group", split_axis=0, concat_axis=0, tiled=True)
    return returned[places]


def solution(mesh):
    return jax.shard_map(
        body,
        mesh=mesh,
        in_specs=(P(("group", "member"), None), P(("group", "member")), P(("group", "member"))),
        out_specs=P(("group", "member")),
        check_vma=False,
    )
```

profile of v0, /device:TPU:0, one launch (start us, length us, event | category | flops | bytes accessed | tf_op | source)
XLA Modules:
  0.0 172.7 jit_solution(3812370682643137008)
XLA Ops:
  6.5 0.7 fusion.17
  7.2 0.7 add_select_fusion
  7.9 1.2 reduce-window.6
  9.1 0.2 slice_reduce_fusion
  9.6 0.7 compare_select_fusion
  10.3 3.6 %scatter_custom_fusion.2 = bf16[1024,768]{1,0:T(8,128)(2,1)S(1)} fusion(s32[512]{0:T(512)S(1)} %compare_select_fusion, bf16[512,768]{1,0:T(8,128)(2,1)} %param.5, bf16[]{:T(256)} %constant.72.clone.1), kind=kCustom, calls=%fused_computation.14 | custom fusion | bytes 1573376 | tf_op jit(solution)/shard_map/scatter | solution.py:64
  13.9 43.1 %all_to_all.45 = bf16[4,256,768]{2,1,0:T(8,128)(2,1)S(1)} all-to-all(bf16[4,256,768]{2,1,0:T(8,128)(2,1)S(1)} %bitcast.47), channel_id=1, replica_groups=mesh['group'=4,'member'=8] {'group'}, dimensions={0} | all-to-all | bytes 3145728 | tf_op jit(solution)/shard_map/all_to_all | solution.py:68
  57.0 0.4 multiply_reduce_fusion
  57.4 1.6 fusion.4
  59.0 3.2 %scatter_custom_fusion.1 = s32[1024]{0:T(1024)} fusion(s32[512]{0:T(512)S(1)} %compare_select_fusion, s32[512]{0:T(512)} %param.7, s32[]{:T(128)} %constant.70.clone.1), kind=kCustom, calls=%fused_computation.32 | custom fusion | bytes 4608 | tf_op jit(solution)/shard_map/scatter | solution.py:66
  62.2 3.2 %all-to-all-start.1 = ((s32[4,256,1]{1,2,0:T(1,128)}), s32[4,256,1]{1,2,0:T(1,128)S(1)}, u32[]{:S(2)}, u32[]{:S(2)}) async-start(s32[4,256,1]{1,2,0:T(1,128)} %bitcast.4), calls=%async_computation.1 | async-start | bytes 8192 | tf_op jit(solution)/shard_map/all_to_all | solution.py:70
  65.5 3.2 %scatter_custom_fusion = s32[1024]{0:T(1024)} fusion(s32[512]{0:T(512)S(1)} %compare_select_fusion, s32[512]{0:T(512)} %param.6, s32[]{:T(128)} %constant.81.clone.1), kind=kCustom, calls=%fused_computation.34 | custom fusion | bytes 4608 | tf_op jit(solution)/shard_map/scatter | solution.py:65
  68.6 2.2 %all-to-all-done.1 = s32[4,256,1]{1,2,0:T(1,128)S(1)} async-done(((s32[4,256,1]{1,2,0:T(1,128)}), s32[4,256,1]{1,2,0:T(1,128)S(1)}, u32[]{:S(2)}, u32[]{:S(2)}) %all-to-all-start.1) | async-done | bytes 4128 | tf_op jit(solution)/shard_map/all_to_all | solution.py:70
  70.8 3.2 %all-to-all-start = ((s32[4,256,1]{1,2,0:T(1,128)}), s32[4,256,1]{1,2,0:T(1,128)S(1)}, u32[]{:S(2)}, u32[]{:S(2)}) async-start(s32[4,256,1]{1,2,0:T(1,128)} %bitcast.2), calls=%async_computation | async-start | bytes 8192 | tf_op jit(solution)/shard_map/all_to_all | solution.py:69
  74.1 9.2 %all_gather.10 = s32[8192]{0:T(1024)S(1)} all-gather(s32[1024]{0:T(1024)S(1)} %bitcast.49), channel_id=1, replica_groups=mesh['group'=4,'member'=8] {'member'}, dimensions={0}, use_global_device_ids=true | all-gather | bytes 36864 | tf_op jit(solution)/shard_map/all_gather | solution.py:81
  83.3 9.0 %all_gather.9 = s32[8192]{0:T(1024)S(1)} all-gather(s32[1024]{0:T(1024)S(1)} %bitcast.51), channel_id=1, replica_groups=mesh['group'=4,'member'=8] {'member'}, dimensions={0}, use_global_device_ids=true | all-gather | bytes 36864 | tf_op jit(solution)/shard_map/all_gather | solution.py:80
  92.3 38.2 %all-gather.2.cloned.1.call-done = bf16[8192,768]{1,0:T(8,128)(2,1)} async-done(((bf16[1024,768]{1,0:T(8,128)(2,1)}), bf16[8192,768]{1,0:T(8,128)(2,1)}) %all-gather.2.cloned.1.call-update) | async-done | bytes 12582928 | tf_op jit(solution)/shard_map/all_gather | solution.py:79
  130.5 21.1 %while.14 = (s32[]{:T(128)}, f32[1024]{0:T(1024)S(1)}, s32[1024]{0:T(1024)S(1)}, s32[8192]{0:T(1024)S(1)}, s32[8192]{0:T(1024)S(1)}, /*index=5*/s32[1024]{0:T(10...) while((s32[]{:T(128)}, f32[1024]{0:T(1024)S(1)}, ...), condition=%wide.region_9.10_spmd.clone, body=%wide.region_7.9_spmd.clone.sunk | while | flops 6467621888 | bytes 7995577 | solution.py:51
  130.6 10.5 %fusion.23 = f32[1024]{0:T(1024)S(1)} fusion(bf16[1024,768]{1,0:T(8,128)(2,1)} %get-tuple-element.274, s32[1024]{0:T(1024)S(1)} %get-tuple-element.272, s32[1024]{0:T(1024)S(1)} %get-tuple-element.269, s32[4096]{0:T(1024)S(1)} %dynamic_slice.32, s32[4096]{0:T(1024)S(1)} %get-tuple-element.241, pred[4096]{0:T(1024)(128)(4,1)S(1)} %get-tuple-element.242, ...), kind=kOutput, calls=%fused_computation.5.clone.1 | convolution fusion | flops 6467615744 | bytes 7913476 | tf_op jit(solution)/shard_map/while/body/eval_jaxpr/dot_general | solution.py:39
  141.2 10.5 %fusion.23 = f32[1024]{0:T(1024)S(1)} fusion(bf16[1024,768]{1,0:T(8,128)(2,1)} %get-tuple-element.274, s32[1024]{0:T(1024)S(1)} %get-tuple-element.272, s32[1024]{0:T(1024)S(1)} %get-tuple-element.269, s32[4096]{0:T(1024)S(1)} %dynamic_slice.32, s32[4096]{0:T(1024)S(1)} %get-tuple-element.241, pred[4096]{0:T(1024)(128)(4,1)S(1)} %get-tuple-element.242, ...), kind=kOutput, calls=%fused_computation.5.clone.1 | convolution fusion | flops 6467615744 | bytes 7913476 | tf_op jit(solution)/shard_map/while/body/eval_jaxpr/dot_general | solution.py:39
  151.7 0.6 broadcast_maximum_fusion
  152.3 4.6 %all-to-all-start.3 = ((f32[4,256,1]{1,2,0:T(1,128)}), f32[4,256,1]{1,2,0:T(1,128)S(1)}, u32[]{:S(2)}, u32[]{:S(2)}) async-start(f32[4,256,1]{1,2,0:T(1,128)} %bitcast.8), calls=%async_computation.3 | async-start | bytes 8192 | tf_op jit(solution)/shard_map/all_to_all | solution.py:85
  156.9 5.6 %all-to-all-done.3 = f32[4,256,1]{1,2,0:T(1,128)S(1)} async-done(((f32[4,256,1]{1,2,0:T(1,128)}), f32[4,256,1]{1,2,0:T(1,128)S(1)}, u32[]{:S(2)}, u32[]{:S(2)}) %all-to-all-start.3) | async-done | bytes 4128 | tf_op jit(solution)/shard_map/all_to_all | solution.py:85
  162.5 3.4 %gather_fusion = f32[512]{0:T(512)} fusion(f32[1024]{0:T(1024)S(1)} %bitcast.46, s32[1024]{0:T(1024)S(1)} %pad_clamp_fusion), kind=kCustom, calls=%fused_computation | custom fusion | bytes 6144 | tf_op jit(solution)/shard_map/gather | solution.py:86
  (17 shorter events, 0.4 us)
Async XLA Ops:
  6.5 124.0 %all-gather.2.cloned.1.call-start = ((), (), s32[]{:S(2)}) async-start(), calls=%async_computation.4 | async-start | bytes 14155776 | tf_op jit(solution)/shard_map/all_gather | solution.py:79
  62.2 8.6 %all-to-all-start.1 = ((s32[4,256,1]{1,2,0:T(1,128)}), s32[4,256,1]{1,2,0:T(1,128)S(1)}, u32[]{:S(2)}, u32[]{:S(2)}) async-start(s32[4,256,1]{1,2,0:T(1,128)} %bitcast.4), calls=%async_computation.1 | async-start | bytes 8192 | tf_op jit(solution)/shard_map/all_to_all | solution.py:70
  70.8 12.4 %all-to-all-start = ((s32[4,256,1]{1,2,0:T(1,128)}), s32[4,256,1]{1,2,0:T(1,128)S(1)}, u32[]{:S(2)}, u32[]{:S(2)}) async-start(s32[4,256,1]{1,2,0:T(1,128)} %bitcast.2), calls=%async_computation | async-start | bytes 8192 | tf_op jit(solution)/shard_map/all_to_all | solution.py:69
  152.3 10.2 %all-to-all-start.3 = ((f32[4,256,1]{1,2,0:T(1,128)}), f32[4,256,1]{1,2,0:T(1,128)S(1)}, u32[]{:S(2)}, u32[]{:S(2)}) async-start(f32[4,256,1]{1,2,0:T(1,128)} %bitcast.8), calls=%async_computation.3 | async-start | bytes 8192 | tf_op jit(solution)/shard_map/all_to_all | solution.py:85
Sparse Core Ops, SparseCore 0:
  59.2 71.3 all-gather.1
where the time goes:
time: 173 us
  blocking collectives  61.3 us (35%)
  waiting for transfers between devices  46 us (27%)
  matrix products  21 us (12%)
  local copies, waits for them, and re-layouts  13.5 us (8%)
  between operations  13.5 us (8%)
  starting transfers between devices  11.1 us (6%)
  other arithmetic  6.23 us (4%)
    all_to_all x1, blocking collectives, body(): lax.all_to_all(send_rows, 'group', split_axis=0, concat_axis=0, tiled=True)  43.1 us
    all_gather x1, waiting for transfers between devices, body(): lax.all_gather(held_units, 'member', axis=0, tiled=True)  38.2 us
    dot_general x2, matrix products, advance(): lax.dot_general(block_units, panel_units, (((1,), (1,)), ((), ())), prefe...  21 us
    all_gather x1, blocking collectives, body(): lax.all_gather(held_ranks, 'member', axis=0, tiled=True)  9.2 us
    all_gather x1, blocking collectives, body(): lax.all_gather(held_ids, 'member', axis=0, tiled=True)  9.03 us
    all_to_all x1, waiting for transfers between devices, body(): lax.all_to_all(best_score, 'group', split_axis=0, concat_axis=0, tiled=True)  5.57 us
    all_to_all x1, starting transfers between devices, body(): lax.all_to_all(best_score, 'group', split_axis=0, concat_axis=0, tiled=True)  4.61 us
    scatter x1, local copies, waits for them, and re-layouts, body(): jnp.zeros((slot_count, features), jnp.bfloat16).at[places].set(embeddings)  3.56 us
  transfers between devices with their start and end apart: 4, of which 3 were waited for; matrix products, arithmetic and copies ran while one was open for 4% of the time, Pallas kernels for 0%

commit v1 on v0

v1 whole, which is shorter than its diff:
```python
import functools
import math

import jax
import jax.numpy as jnp
from jax import lax
from jax.experimental import pallas as pl
from jax.experimental.pallas import tpu as pltpu
from jax.sharding import PartitionSpec as P

META = 128


def flip(index, mask):
    result = index
    bit = 1
    while bit <= mask:
        if mask & bit:
            result = result + bit - 2 * bit * lax.rem(lax.div(index, bit), 2)
        bit *= 2
    return result


def kernel(
    groups,
    members,
    emb_ref,
    ids_ref,
    ranks_ref,
    out_ref,
    packed,
    send1,
    recv1,
    send2,
    held,
    score2,
    back2,
    score1,
    back1,
    s1_send,
    s1_recv,
    s2_send,
    s2_recv,
    ag_send,
    ag_recv,
    b2_send,
    b2_recv,
    b1_send,
    b1_recv,
):
    rows, features = emb_ref.shape
    width = features + META
    deal = rows // members
    share = rows // groups
    z = lax.axis_index("group")
    m = lax.axis_index("member")

    barrier = pltpu.get_barrier_semaphore()
    for r in range(1, members):
        pl.semaphore_signal(
            barrier, inc=1, device_id=(z, flip(m, r)), device_id_type=pl.DeviceIdType.MESH
        )
    for d in range(1, groups):
        pl.semaphore_signal(
            barrier, inc=1, device_id=(flip(z, d), m), device_id_type=pl.DeviceIdType.MESH
        )

    def push(src, dst, send_sem, recv_sem, where):
        copy = pltpu.make_async_remote_copy(
            src_ref=src,
            dst_ref=dst,
            send_sem=send_sem,
            recv_sem=recv_sem,
            device_id=where,
            device_id_type=pl.DeviceIdType.MESH,
        )
        copy.start()
        return copy

    def column(row):
        return jnp.broadcast_to(row, (8, rows)).T[:, 0:1]

    sub = lax.broadcasted_iota(jnp.int32, (rows, rows), 0)
    lane = lax.broadcasted_iota(jnp.int32, (1, rows), 1)

    def order(bucket_row):
        key_row = (bucket_row * rows + lane).astype(jnp.float32)
        key_col = column(key_row)
        return jnp.sum((key_col < key_row).astype(jnp.float32), axis=0, keepdims=True).astype(
            jnp.int32
        )

    widened = emb_ref[...].astype(jnp.float32)
    square = jnp.mean(widened * widened, axis=-1, keepdims=True)
    packed[:, :features] = (
        widened * lax.rsqrt(square + 1e-06) * (1.0 / math.sqrt(features))
    ).astype(jnp.bfloat16)
    ids = ids_ref[...]
    ranks = ranks_ref[...]
    residue = lax.rem(ids, groups)
    level = lax.broadcasted_iota(jnp.int32, (META, rows), 0)
    high = lax.div(ranks, 256)
    fields = jnp.where(
        level == 0,
        ids,
        jnp.where(
            level == 1,
            high,
            jnp.where(level == 2, ranks - high * 256, jnp.where(level == 3, residue, 0)),
        ),
    )
    packed[:, features:] = fields.astype(jnp.float32).T.astype(jnp.bfloat16)

    place = order(residue)
    slot1 = jnp.bitwise_xor(lax.rem(place, members), m) * deal + lax.div(place, members)
    send1[...] = jnp.dot(
        (sub == slot1).astype(jnp.float32).astype(jnp.bfloat16),
        packed[...],
        preferred_element_type=jnp.float32,
    ).astype(jnp.bfloat16)
    pl.semaphore_wait(barrier, members + groups - 2)
    copies1 = [
        push(
            send1.at[pl.ds(r * deal, deal)],
            recv1.at[pl.ds(r * deal, deal)],
            s1_send.at[r],
            s1_recv.at[r],
            (z, flip(m, r)),
        )
        for r in range(members - 1, 0, -1)
    ]
    recv1[:deal] = send1[:deal]
    for copy in copies1:
        copy.wait_recv()

    residue2 = recv1[:, features:].astype(jnp.float32).T[3:4].astype(jnp.int32)
    slot2 = order(jnp.bitwise_xor(residue2, z))
    send2[...] = jnp.dot(
        (sub == slot2).astype(jnp.float32).astype(jnp.bfloat16),
        recv1[...],
        preferred_element_type=jnp.float32,
    ).astype(jnp.bfloat16)
    copies2 = {
        d: push(
            send2.at[pl.ds(d * share, share)],
            held.at[0, pl.ds(d * share, share)],
            s2_send.at[d],
            s2_recv.at[d],
            (flip(z, d), m),
        )
        for d in range(groups - 1, 0, -1)
    }
    held[0, :share] = send2[:share]

    gathers = {}
    half = share // 2

    def forward(source, slot, d, part, hop):
        start = d * share + (0 if part is None else part * half)
        span = pl.ds(start, share if part is None else half)
        index = (slot, d, part or 0)
        gathers[(slot, d, part)] = push(
            held.at[source, span],
            held.at[slot, span],
            ag_send.at[index],
            ag_recv.at[index],
            (z, flip(m, hop)),
        )

    def arrive(slot, d, part=None):
        gathers[(slot, d, part)].wait_recv()

    tree = members == 8 and groups == 4

    def own_chunk(d):
        if d:
            copies2[d].wait_recv()
        for r in (2, 4, 1) if tree else range(1, members):
            forward(0, r, d, None, r)

    def pass_on(d):
        arrive(2, d)
        forward(2, 6, d, 0, 4)
        forward(2, 3, d, None, 1)
        arrive(4, d)
        forward(4, 6, d, 1, 2)
        forward(4, 5, d, None, 1)

    def pass_diagonal(d):
        for part in (0, 1):
            arrive(6, d, part)
            forward(6, 7, d, part, 1)

    for d in range(groups):
        own_chunk(d)
        if tree and d >= 1:
            pass_on(d - 1)
        if tree and d >= 2:
            pass_diagonal(d - 2)

    query_fields = held[0, :, features:].astype(jnp.float32).T
    query_low = query_fields[0:1] * 65536.0
    query_key = query_low + query_fields[1:2] * 256.0 + query_fields[2:3]

    def scored(r, best):
        scores = lax.dot_general(
            held[r, :, :features],
            held[0, :, :features],
            (((1,), (1,)), ((), ())),
            preferred_element_type=jnp.float32,
        )
        fields = held[r, :, features:].astype(jnp.float32)
        key = fields[:, 0:1] * 65536.0 + fields[:, 1:2] * 256.0 + fields[:, 2:3]
        allowed = (key >= query_low) & (key < query_key)
        return jnp.maximum(
            best, jnp.max(jnp.where(allowed, scores, -1.0), axis=0, keepdims=True)
        )

    best = jnp.full((1, rows), -1.0, jnp.float32)
    if tree:
        pass_on(groups - 1)
        pass_diagonal(groups - 2)
        best = scored(0, best)
        for r in (2, 4):
            best = scored(r, best)
        pass_diagonal(groups - 1)
        for r in (1, 3, 5):
            for d in range(groups):
                arrive(r, d)
            best = scored(r, best)
        best = scored(6, best)
        for d in range(groups):
            for part in (0, 1):
                arrive(7, d, part)
        best = scored(7, best)
    else:
        best = scored(0, best)
        for r in range(1, members):
            for d in range(groups):
                arrive(r, d)
            best = scored(r, best)

    score2[...] = best
    home2 = [
        push(score2, back2.at[d], b2_send.at[d], b2_recv.at[d], (flip(z, d), m))
        for d in range(groups - 1, 0, -1)
    ]
    for copy in home2:
        copy.wait_recv()
    merged = best
    for d in range(1, groups):
        merged = jnp.where(lax.div(lane, share) == d, back2[d], merged)
    best = jnp.max(jnp.where(sub == slot2, column(merged), -2.0), axis=0, keepdims=True)
    score1[...] = best
    home1 = [
        push(score1, back1.at[r], b1_send.at[r], b1_recv.at[r], (z, flip(m, r)))
        for r in range(members - 1, 0, -1)
    ]
    for copy in home1:
        copy.wait_recv()
    merged = best
    for r in range(1, members):
        merged = jnp.where(lax.div(lane, deal) == r, back1[r], merged)
    out_ref[...] = jnp.max(jnp.where(sub == slot1, column(merged), -2.0), axis=0, keepdims=True)

    for copy in [*copies1, *copies2.values(), *gathers.values(), *home2, *home1]:
        copy.wait_send()


def body(embeddings, cluster_ids, ranks):
    rows, features = embeddings.shape
    groups = lax.axis_size("group")
    members = lax.axis_size("member")
    width = features + META
    scores = pl.pallas_call(
        functools.partial(kernel, groups, members),
        out_shape=jax.ShapeDtypeStruct((1, rows), jnp.float32),
        in_specs=[pl.BlockSpec(memory_space=pltpu.VMEM)] * 3,
        out_specs=pl.BlockSpec(memory_space=pltpu.VMEM),
        scratch_shapes=[
            pltpu.VMEM((rows, width), jnp.bfloat16),
            pltpu.VMEM((rows, width), jnp.bfloat16),
            pltpu.VMEM((rows, width), jnp.bfloat16),
            pltpu.VMEM((rows, width), jnp.bfloat16),
            pltpu.VMEM((members, rows, width), jnp.bfloat16),
            pltpu.VMEM((1, rows), jnp.float32),
            pltpu.VMEM((groups, 1, rows), jnp.float32),
            pltpu.VMEM((1, rows), jnp.float32),
            pltpu.VMEM((members, 1, rows), jnp.float32),
            pltpu.SemaphoreType.DMA((members,)),
            pltpu.SemaphoreType.DMA((members,)),
            pltpu.SemaphoreType.DMA((groups,)),
            pltpu.SemaphoreType.DMA((groups,)),
            pltpu.SemaphoreType.DMA((members, groups, 2)),
            pltpu.SemaphoreType.DMA((members, groups, 2)),
            pltpu.SemaphoreType.DMA((groups,)),
            pltpu.SemaphoreType.DMA((groups,)),
            pltpu.SemaphoreType.DMA((members,)),
            pltpu.SemaphoreType.DMA((members,)),
        ],
        compiler_params=pltpu.CompilerParams(
            collective_id=0, has_side_effects=True, vmem_limit_bytes=48 * 1024 * 1024
        ),
    )(embeddings, cluster_ids.reshape(1, rows), ranks.reshape(1, rows))
    return scores.reshape(rows)


def solution(mesh):
    return jax.shard_map(
        body,
        mesh=mesh,
        in_specs=(P(("group", "member"), None), P(("group", "member")), P(("group", "member"))),
        out_specs=P(("group", "member")),
        check_vma=False,
    )
```

time: 173 us -> 76 us (0.44)
  Pallas kernels: 0 us -> 72.8 us
  blocking collectives: 61.3 us -> 0 us
  waiting for transfers between devices: 46 us -> 0 us
  matrix products: 21 us -> 0 us
  between operations: 13.5 us -> 0.01 us
  starting transfers between devices: 11.1 us -> 0 us
  local copies, waits for them, and re-layouts: 13.5 us -> 3.08 us
  other arithmetic: 6.23 us -> 0 us
    pallas_call x0 -> x1, Pallas kernels: none -> 72.8 us  [body(): pl.pallas_call(functools.partial(kernel, groups, members), out_shape=jax....]
    all_to_all x1 -> x0, blocking collectives: 43.1 us -> none  [body(): lax.all_to_all(send_rows, 'group', split_axis=0, concat_axis=0, tiled=True)]
    all_gather x1 -> x0, waiting for transfers between devices: 38.2 us -> none  [body(): lax.all_gather(held_units, 'member', axis=0, tiled=True)]
    dot_general x2 -> x0, matrix products: 21 us -> none  [advance(): lax.dot_general(block_units, panel_units, (((1,), (1,)), ((), ())), prefe...]
    all_gather x2 -> x0, blocking collectives: 18.2 us -> none  [the longest x1 9.2 us: body(): lax.all_gather(held_ranks, 'member', axis=0, tiled=True)]
    all_to_all x3 -> x0, starting transfers between devices: 11.1 us -> none  [the longest x1 4.61 us: body(): lax.all_to_all(best_score, 'group', split_axis=0, concat_axis=0, tiled=True)]
    scatter x3 -> x0, local copies, waits for them, and re-layouts: 9.9 us -> none  [the longest x1 3.56 us: body(): jnp.zeros((slot_count, features), jnp.bfloat16).at[places].set(embeddings)]
    all_to_all x3 -> x0, waiting for transfers between devices: 7.77 us -> none  [the longest x1 5.57 us: body(): lax.all_to_all(best_score, 'group', split_axis=0, concat_axis=0, tiled=True)]
  transfers between devices with their start and end apart: 4 -> 0, of which waited for: 3 -> 0; matrix products, arithmetic and copies ran while one was open for 4% -> 0% of each run, Pallas kernels for 0% -> 0%
where the time goes in v1:
time: 76 us; the launch traced here: 75.8 us
  Pallas kernels  72.8 us (96%)
  local copies, waits for them, and re-layouts  3.08 us (4%)
    pallas_call x1, Pallas kernels, body(): pl.pallas_call(functools.partial(kernel, groups, members), out_shape=jax....  72.8 us
    unnamed x7, local copies, waits for them, and re-layouts  3.08 us

profile of v1, /device:TPU:0, one launch (start us, length us, event | category | flops | bytes accessed | tf_op | source)
XLA Modules:
  0.0 75.8 jit_solution(17532372449270709034)
XLA Ops:
  0.0 0.0 copy-start.1
  0.0 0.7 copy-done.1
  0.7 0.0 copy-start
  0.7 1.1 %copy-done = bf16[512,768]{1,0:T(8,128)(2,1)S(1)} copy-done((bf16[512,768]{1,0:T(8,128)(2,1)S(1)}, bf16[512,768]{1,0:T(8,128)(2,1)}, u32[]{:S(2)}) %copy-start) | copy-done | bytes 786456
  1.8 0.0 copy-start.2
  1.8 0.7 copy-done.2
  2.5 72.8 %shard_map.37 = f32[1,512]{1,0:T(1,128)S(1)} custom-call(bf16[512,768]{1,0:T(8,128)(2,1)S(1)} %copy-done, s32[1,512]{1,0:T(1,128)S(1)} %bitcast.4, s32[1,512]{1,0:T(1,128)S(1)} %bitcast.5), custom_call_target="tpu_custom_call" | custom-call | tf_op jit(solution)/shard_map/pallas_call | solution.py:275
  75.3 0.6 copy.5
Async XLA Ops:
  0.0 0.7 copy-start.1
  0.7 1.1 %copy-start = (bf16[512,768]{1,0:T(8,128)(2,1)S(1)}, bf16[512,768]{1,0:T(8,128)(2,1)}, u32[]{:S(2)}) copy-start(bf16[512,768]{1,0:T(8,128)(2,1)} %emb_ref.1) | copy-start | bytes 2359300
  1.8 0.7 copy-start.2

commit v2 on v1

--- a/solution.py
+++ b/solution.py
@@ -7,8 +7,6 @@
 from jax.experimental import pallas as pl
 from jax.experimental.pallas import tpu as pltpu
 from jax.sharding import PartitionSpec as P
-
-META = 128
 
 
 def flip(index, mask):
@@ -28,33 +26,55 @@
     ids_ref,
     ranks_ref,
     out_ref,
+    emb,
+    ids_row,
+    ranks_row,
     packed,
     send1,
     recv1,
     send2,
     held,
+    key1,
+    keyin1,
+    key2,
+    keyin2,
+    keys,
     score2,
     back2,
     score1,
     back1,
+    local,
     s1_send,
     s1_recv,
     s2_send,
     s2_recv,
     ag_send,
     ag_recv,
+    k1_send,
+    k1_recv,
+    k2_send,
+    k2_recv,
+    k3_send,
+    k3_recv,
     b2_send,
     b2_recv,
     b1_send,
     b1_recv,
 ):
     rows, features = emb_ref.shape
-    width = features + META
     deal = rows // members
     share = rows // groups
     z = lax.axis_index("group")
     m = lax.axis_index("member")
 
+    loads = [
+        pltpu.make_async_copy(src, dst, local.at[n])
+        for n, (src, dst) in enumerate(
+            ((ids_ref, ids_row), (ranks_ref, ranks_row), (emb_ref, emb))
+        )
+    ]
+    for load in loads:
+        load.start()
     barrier = pltpu.get_barrier_semaphore()
     for r in range(1, members):
         pl.semaphore_signal(
@@ -90,35 +110,43 @@
             jnp.int32
         )
 
-    widened = emb_ref[...].astype(jnp.float32)
+    def permutation(slot):
+        return (sub == slot).astype(jnp.float32).astype(jnp.bfloat16)
+
+    def place_keys(ids, ranks, chosen):
+        level = lax.broadcasted_iota(jnp.int32, (16, rows), 0)
+        high = lax.div(ranks, 256)
+        fields = jnp.where(
+            level == 0, ids, jnp.where(level == 1, high, jnp.where(level == 2, ranks - high * 256, 0))
+        )
+        placed = lax.dot_general(
+            fields.astype(jnp.float32).astype(jnp.bfloat16),
+            chosen,
+            (((1,), (1,)), ((), ())),
+            preferred_element_type=jnp.float32,
+        )
+        return placed[0:1] * 65536.0 + placed[1:2] * 256.0 + placed[2:3]
+
+    loads[0].wait()
+    loads[1].wait()
+    ids = ids_row[...]
+    place = order(lax.rem(ids, groups))
+    slot1 = jnp.bitwise_xor(lax.rem(place, members), m) * deal + lax.div(place, members)
+    chosen1 = permutation(slot1)
+    key1[...] = place_keys(ids, ranks_row[...], chosen1)
+    loads[2].wait()
+    widened = emb[...].astype(jnp.float32)
     square = jnp.mean(widened * widened, axis=-1, keepdims=True)
-    packed[:, :features] = (
-        widened * lax.rsqrt(square + 1e-06) * (1.0 / math.sqrt(features))
-    ).astype(jnp.bfloat16)
-    ids = ids_ref[...]
-    ranks = ranks_ref[...]
-    residue = lax.rem(ids, groups)
-    level = lax.broadcasted_iota(jnp.int32, (META, rows), 0)
-    high = lax.div(ranks, 256)
-    fields = jnp.where(
-        level == 0,
-        ids,
-        jnp.where(
-            level == 1,
-            high,
-            jnp.where(level == 2, ranks - high * 256, jnp.where(level == 3, residue, 0)),
-        ),
+    packed[...] = (widened * lax.rsqrt(square + 1e-06) * (1.0 / math.sqrt(features))).astype(
+        jnp.bfloat16
     )
-    packed[:, features:] = fields.astype(jnp.float32).T.astype(jnp.bfloat16)
-
-    place = order(residue)
-    slot1 = jnp.bitwise_xor(lax.rem(place, members), m) * deal + lax.div(place, members)
-    send1[...] = jnp.dot(
-        (sub == slot1).astype(jnp.float32).astype(jnp.bfloat16),
-        packed[...],
-        preferred_element_type=jnp.float32,
-    ).astype(jnp.bfloat16)
+    send1[...] = jnp.dot(chosen1, packed[...], preferred_element_type=jnp.float32).astype(
+        jnp.bfloat16
+    )
     pl.semaphore_wait(barrier, members + groups - 2)
+    small = []
+    for r in range(1, members):
+        small.append(push(key1, keyin1.at[r], k1_send.at[r], k1_recv.at[r], (z, flip(m, r))))
     copies1 = [
         push(
             send1.at[pl.ds(r * deal, deal)],
@@ -130,16 +158,25 @@
         for r in range(members - 1, 0, -1)
     ]
     recv1[:deal] = send1[:deal]
+
+    merged = key1[...]
+    for r in range(1, members):
+        small[r - 1].wait_recv()
+        merged = jnp.where(lax.div(lane, deal) == r, keyin1[r], merged)
+    merged = merged.astype(jnp.int32)
+    ids = lax.div(merged, 65536)
+    slot2 = order(jnp.bitwise_xor(lax.rem(ids, groups), z))
+    chosen2 = permutation(slot2)
+    key2[...] = place_keys(ids, merged - ids * 65536, chosen2)
+    small2 = [
+        push(key2, keyin2.at[d], k2_send.at[d], k2_recv.at[d], (flip(z, d), m))
+        for d in range(1, groups)
+    ]
     for copy in copies1:
         copy.wait_recv()
-
-    residue2 = recv1[:, features:].astype(jnp.float32).T[3:4].astype(jnp.int32)
-    slot2 = order(jnp.bitwise_xor(residue2, z))
-    send2[...] = jnp.dot(
-        (sub == slot2).astype(jnp.float32).astype(jnp.bfloat16),
-        recv1[...],
-        preferred_element_type=jnp.float32,
-    ).astype(jnp.bfloat16)
+    send2[...] = jnp.dot(chosen2, recv1[...], preferred_element_type=jnp.float32).astype(
+        jnp.bfloat16
+    )
     copies2 = {
         d: push(
             send2.at[pl.ds(d * share, share)],
@@ -148,7 +185,7 @@
             s2_recv.at[d],
             (flip(z, d), m),
         )
-        for d in range(groups - 1, 0, -1)
+        for d in range(1, groups)
     }
     held[0, :share] = send2[:share]
 
@@ -191,26 +228,33 @@
             arrive(6, d, part)
             forward(6, 7, d, part, 1)
 
-    for d in range(groups):
+    own_chunk(0)
+    merged = key2[...]
+    for d in range(1, groups):
+        small2[d - 1].wait_recv()
+        merged = jnp.where(lax.div(lane, share) == d, keyin2[d], merged)
+    keys[0] = merged
+    small3 = [
+        push(keys.at[0], keys.at[r], k3_send.at[r], k3_recv.at[r], (z, flip(m, r)))
+        for r in range(1, members)
+    ]
+    query_key = merged
+    query_low = (lax.div(merged.astype(jnp.int32), 65536) * 65536).astype(jnp.float32)
+
+    for d in range(1, groups):
         own_chunk(d)
-        if tree and d >= 1:
+        if tree:
             pass_on(d - 1)
         if tree and d >= 2:
             pass_diagonal(d - 2)
-
-    query_fields = held[0, :, features:].astype(jnp.float32).T
-    query_low = query_fields[0:1] * 65536.0
-    query_key = query_low + query_fields[1:2] * 256.0 + query_fields[2:3]
+    for copy in small3:
+        copy.wait_recv()
 
     def scored(r, best):
         scores = lax.dot_general(
-            held[r, :, :features],
-            held[0, :, :features],
-            (((1,), (1,)), ((), ())),
-            preferred_element_type=jnp.float32,
-        )
-        fields = held[r, :, features:].astype(jnp.float32)
-        key = fields[:, 0:1] * 65536.0 + fields[:, 1:2] * 256.0 + fields[:, 2:3]
+            held[r], held[0], (((1,), (1,)), ((), ())), preferred_element_type=jnp.float32
+        )
+        key = column(keys[r])
         allowed = (key >= query_low) & (key < query_key)
         return jnp.maximum(
             best, jnp.max(jnp.where(allowed, scores, -1.0), axis=0, keepdims=True)
@@ -263,7 +307,16 @@
         merged = jnp.where(lax.div(lane, deal) == r, back1[r], merged)
     out_ref[...] = jnp.max(jnp.where(sub == slot1, column(merged), -2.0), axis=0, keepdims=True)
 
-    for copy in [*copies1, *copies2.values(), *gathers.values(), *home2, *home1]:
+    for copy in [
+        *small,
+        *copies1,
+        *small2,
+        *copies2.values(),
+        *small3,
+        *gathers.values(),
+        *home2,
+        *home1,
+    ]:
         copy.wait_send()
 
 
@@ -271,28 +324,42 @@
     rows, features = embeddings.shape
     groups = lax.axis_size("group")
     members = lax.axis_size("member")
-    width = features + META
     scores = pl.pallas_call(
         functools.partial(kernel, groups, members),
         out_shape=jax.ShapeDtypeStruct((1, rows), jnp.float32),
-        in_specs=[pl.BlockSpec(memory_space=pltpu.VMEM)] * 3,
+        in_specs=[pl.BlockSpec(memory_space=pl.ANY)] * 3,
         out_specs=pl.BlockSpec(memory_space=pltpu.VMEM),
         scratch_shapes=[
-            pltpu.VMEM((rows, width), jnp.bfloat16),
-            pltpu.VMEM((rows, width), jnp.bfloat16),
-            pltpu.VMEM((rows, width), jnp.bfloat16),
-            pltpu.VMEM((rows, width), jnp.bfloat16),
-            pltpu.VMEM((members, rows, width), jnp.bfloat16),
+            pltpu.VMEM((rows, features), jnp.bfloat16),
+            pltpu.VMEM((1, rows), jnp.int32),
+            pltpu.VMEM((1, rows), jnp.int32),
+            pltpu.VMEM((rows, features), jnp.bfloat16),
+            pltpu.VMEM((rows, features), jnp.bfloat16),
+            pltpu.VMEM((rows, features), jnp.bfloat16),
+            pltpu.VMEM((rows, features), jnp.bfloat16),
+            pltpu.VMEM((members, rows, features), jnp.bfloat16),
+            pltpu.VMEM((1, rows), jnp.float32),
+            pltpu.VMEM((members, 1, rows), jnp.float32),
+            pltpu.VMEM((1, rows), jnp.float32),
+            pltpu.VMEM((groups, 1, rows), jnp.float32),
+            pltpu.VMEM((members, 1, rows), jnp.float32),
             pltpu.VMEM((1, rows), jnp.float32),
             pltpu.VMEM((groups, 1, rows), jnp.float32),
             pltpu.VMEM((1, rows), jnp.float32),
             pltpu.VMEM((members, 1, rows), jnp.float32),
+            pltpu.SemaphoreType.DMA((3,)),
             pltpu.SemaphoreType.DMA((members,)),
             pltpu.SemaphoreType.DMA((members,)),
             pltpu.SemaphoreType.DMA((groups,)),
             pltpu.SemaphoreType.DMA((groups,)),
             pltpu.SemaphoreType.DMA((members, groups, 2)),
             pltpu.SemaphoreType.DMA((members, groups, 2)),
+            pltpu.SemaphoreType.DMA((members,)),
+            pltpu.SemaphoreType.DMA((members,)),
+            pltpu.SemaphoreType.DMA((groups,)),
+            pltpu.SemaphoreType.DMA((groups,)),
+            pltpu.SemaphoreType.DMA((members,)),
+            pltpu.SemaphoreType.DMA((members,)),
             pltpu.SemaphoreType.DMA((groups,)),
             pltpu.SemaphoreType.DMA((groups,)),
             pltpu.SemaphoreType.DMA((members,)),

time: 76 us -> 65 us (0.86)
  Pallas kernels: 72.8 us -> 61.7 us
    pallas_call x1, Pallas kernels: 72.8 us -> 61.7 us  [body(): pl.pallas_call(functools.partial(kernel, groups, members), out_shape=jax....]
where the time goes in v2:
time: 65 us; the launch traced here: 64.8 us
  Pallas kernels  61.7 us (95%)
  local copies, waits for them, and re-layouts  3.08 us (5%)
    pallas_call x1, Pallas kernels, body(): pl.pallas_call(functools.partial(kernel, groups, members), out_shape=jax....  61.7 us
    unnamed x7, local copies, waits for them, and re-layouts  3.08 us

profile of v2, /device:TPU:0, one launch (start us, length us, event | category | flops | bytes accessed | tf_op | source)
XLA Modules:
  0.0 64.8 jit_solution(12319154120681156204)
XLA Ops:
  0.0 0.0 copy-start.1
  0.0 0.7 %copy-done.1 = s32[512]{0:T(512)S(1)} copy-done((s32[512]{0:T(512)S(1)}, s32[512]{0:T(512)}, u32[]{:S(2)}) %copy-start.1) | copy-done | bytes 2072
  0.7 0.0 copy-start
  0.7 1.1 %copy-done = bf16[512,768]{1,0:T(8,128)(2,1)S(1)} copy-done((bf16[512,768]{1,0:T(8,128)(2,1)S(1)}, bf16[512,768]{1,0:T(8,128)(2,1)}, u32[]{:S(2)}) %copy-start) | copy-done | bytes 786456
  1.8 0.0 copy-start.2
  1.8 0.7 %copy-done.2 = s32[512]{0:T(512)S(1)} copy-done((s32[512]{0:T(512)S(1)}, s32[512]{0:T(512)}, u32[]{:S(2)}) %copy-start.2) | copy-done | bytes 2072
  2.5 61.7 %shard_map.37 = f32[1,512]{1,0:T(1,128)S(1)} custom-call(bf16[512,768]{1,0:T(8,128)(2,1)S(1)} %copy-done, s32[1,512]{1,0:T(1,128)S(1)} %bitcast.4, s32[1,512]{1,0:T(1,128)S(1)} %bitcast.5), custom_call_target="tpu_custom_call" | custom-call | tf_op jit(solution)/shard_map/pallas_call | solution.py:327
  64.3 0.6 copy.5
Async XLA Ops:
  0.0 0.7 %copy-start.1 = (s32[512]{0:T(512)S(1)}, s32[512]{0:T(512)}, u32[]{:S(2)}) copy-start(s32[512]{0:T(512)} %param.4) | copy-start | bytes 6148
  0.7 1.1 %copy-start = (bf16[512,768]{1,0:T(8,128)(2,1)S(1)}, bf16[512,768]{1,0:T(8,128)(2,1)}, u32[]{:S(2)}) copy-start(bf16[512,768]{1,0:T(8,128)(2,1)} %emb_ref.1) | copy-start | bytes 2359300
  1.8 0.7 %copy-start.2 = (s32[512]{0:T(512)S(1)}, s32[512]{0:T(512)}, u32[]{:S(2)}) copy-start(s32[512]{0:T(512)} %param.5) | copy-start | bytes 6148

commit v3 on v2

--- a/solution.py
+++ b/solution.py
@@ -7,6 +7,8 @@
 from jax.experimental import pallas as pl
 from jax.experimental.pallas import tpu as pltpu
 from jax.sharding import PartitionSpec as P
+
+HALVES = 2
 
 
 def flip(index, mask):
@@ -62,8 +64,9 @@
     b1_recv,
 ):
     rows, features = emb_ref.shape
-    deal = rows // members
-    share = rows // groups
+    part = rows // HALVES
+    deal = part // members
+    share = part // groups
     z = lax.axis_index("group")
     m = lax.axis_index("member")
 
@@ -98,7 +101,7 @@
         return copy
 
     def column(row):
-        return jnp.broadcast_to(row, (8, rows)).T[:, 0:1]
+        return jnp.broadcast_to(row, (8, row.shape[1])).T[:, 0:1]
 
     sub = lax.broadcasted_iota(jnp.int32, (rows, rows), 0)
     lane = lax.broadcasted_iota(jnp.int32, (1, rows), 1)
@@ -131,7 +134,11 @@
     loads[1].wait()
     ids = ids_row[...]
     place = order(lax.rem(ids, groups))
-    slot1 = jnp.bitwise_xor(lax.rem(place, members), m) * deal + lax.div(place, members)
+    slot1 = (
+        lax.rem(lax.div(place, members), HALVES) * part
+        + jnp.bitwise_xor(lax.rem(place, members), m) * deal
+        + lax.div(place, members * HALVES)
+    )
     chosen1 = permutation(slot1)
     key1[...] = place_keys(ids, ranks_row[...], chosen1)
     loads[2].wait()
@@ -147,56 +154,65 @@
     small = []
     for r in range(1, members):
         small.append(push(key1, keyin1.at[r], k1_send.at[r], k1_recv.at[r], (z, flip(m, r))))
-    copies1 = [
-        push(
-            send1.at[pl.ds(r * deal, deal)],
-            recv1.at[pl.ds(r * deal, deal)],
-            s1_send.at[r],
-            s1_recv.at[r],
+    copies1 = {
+        (h, r): push(
+            send1.at[pl.ds(h * part + r * deal, deal)],
+            recv1.at[pl.ds(h * part + r * deal, deal)],
+            s1_send.at[h, r],
+            s1_recv.at[h, r],
             (z, flip(m, r)),
         )
+        for h in range(HALVES)
         for r in range(members - 1, 0, -1)
-    ]
-    recv1[:deal] = send1[:deal]
+    }
+    for h in range(HALVES):
+        recv1[h * part : h * part + deal] = send1[h * part : h * part + deal]
 
     merged = key1[...]
     for r in range(1, members):
         small[r - 1].wait_recv()
-        merged = jnp.where(lax.div(lane, deal) == r, keyin1[r], merged)
+        merged = jnp.where(lax.div(lax.rem(lane, part), deal) == r, keyin1[r], merged)
     merged = merged.astype(jnp.int32)
     ids = lax.div(merged, 65536)
-    slot2 = order(jnp.bitwise_xor(lax.rem(ids, groups), z))
+    slot2 = order(lax.div(lane, part) * groups + jnp.bitwise_xor(lax.rem(ids, groups), z))
     chosen2 = permutation(slot2)
     key2[...] = place_keys(ids, merged - ids * 65536, chosen2)
     small2 = [
         push(key2, keyin2.at[d], k2_send.at[d], k2_recv.at[d], (flip(z, d), m))
         for d in range(1, groups)
     ]
-    for copy in copies1:
-        copy.wait_recv()
-    send2[...] = jnp.dot(chosen2, recv1[...], preferred_element_type=jnp.float32).astype(
-        jnp.bfloat16
-    )
-    copies2 = {
-        d: push(
-            send2.at[pl.ds(d * share, share)],
-            held.at[0, pl.ds(d * share, share)],
-            s2_send.at[d],
-            s2_recv.at[d],
-            (flip(z, d), m),
-        )
-        for d in range(1, groups)
-    }
-    held[0, :share] = send2[:share]
+    copies2 = {}
+
+    def exchange(h):
+        for r in range(1, members):
+            copies1[(h, r)].wait_recv()
+        first = h * part
+        send2[first : first + part] = jnp.dot(
+            chosen2[first : first + part, first : first + part],
+            recv1[first : first + part],
+            preferred_element_type=jnp.float32,
+        ).astype(jnp.bfloat16)
+        for d in range(1, groups):
+            span = pl.ds(first + d * share, share)
+            copies2[(h, d)] = push(
+                send2.at[span],
+                held.at[0, span],
+                s2_send.at[h, d],
+                s2_recv.at[h, d],
+                (flip(z, d), m),
+            )
+        held[0, first : first + share] = send2[first : first + share]
 
     gathers = {}
+    arrived = set()
     half = share // 2
 
-    def forward(source, slot, d, part, hop):
-        start = d * share + (0 if part is None else part * half)
-        span = pl.ds(start, share if part is None else half)
-        index = (slot, d, part or 0)
-        gathers[(slot, d, part)] = push(
+    def forward(source, slot, chunk, side, hop):
+        h, d = chunk
+        start = h * part + d * share + (0 if side is None else side * half)
+        span = pl.ds(start, share if side is None else half)
+        index = (slot, h * groups + d, side or 0)
+        gathers[(slot, chunk, side)] = push(
             held.at[source, span],
             held.at[slot, span],
             ag_send.at[index],
@@ -204,35 +220,41 @@
             (z, flip(m, hop)),
         )
 
-    def arrive(slot, d, part=None):
-        gathers[(slot, d, part)].wait_recv()
+    def arrive(slot, chunk, side=None):
+        if (slot, chunk, side) not in arrived:
+            gathers[(slot, chunk, side)].wait_recv()
+            arrived.add((slot, chunk, side))
 
     tree = members == 8 and groups == 4
 
-    def own_chunk(d):
-        if d:
-            copies2[d].wait_recv()
+    def own_chunk(chunk):
+        if chunk[1]:
+            copies2[chunk].wait_recv()
         for r in (2, 4, 1) if tree else range(1, members):
-            forward(0, r, d, None, r)
-
-    def pass_on(d):
-        arrive(2, d)
-        forward(2, 6, d, 0, 4)
-        forward(2, 3, d, None, 1)
-        arrive(4, d)
-        forward(4, 6, d, 1, 2)
-        forward(4, 5, d, None, 1)
-
-    def pass_diagonal(d):
-        for part in (0, 1):
-            arrive(6, d, part)
-            forward(6, 7, d, part, 1)
-
-    own_chunk(0)
+            forward(0, r, chunk, None, r)
+
+    def pass_on(chunk):
+        arrive(2, chunk)
+        forward(2, 6, chunk, 0, 4)
+        forward(2, 3, chunk, None, 1)
+        arrive(4, chunk)
+        forward(4, 6, chunk, 1, 2)
+        forward(4, 5, chunk, None, 1)
+
+    def pass_diagonal(chunk):
+        for side in (0, 1):
+            arrive(6, chunk, side)
+            forward(6, 7, chunk, side, 1)
+
+    chunks = [(h, 0) for h in range(HALVES)]
+    chunks += [(h, d) for h in range(HALVES) for d in range(1, groups)]
+    for h in range(HALVES):
+        exchange(h)
+        own_chunk((h, 0))
     merged = key2[...]
     for d in range(1, groups):
         small2[d - 1].wait_recv()
-        merged = jnp.where(lax.div(lane, share) == d, keyin2[d], merged)
+        merged = jnp.where(lax.div(lax.rem(lane, part), share) == d, keyin2[d], merged)
     keys[0] = merged
     small3 = [
         push(keys.at[0], keys.at[r], k3_send.at[r], k3_recv.at[r], (z, flip(m, r)))
@@ -241,48 +263,49 @@
     query_key = merged
     query_low = (lax.div(merged.astype(jnp.int32), 65536) * 65536).astype(jnp.float32)
 
-    for d in range(1, groups):
-        own_chunk(d)
+    if tree:
+        pass_on(chunks[0])
+    for n in range(HALVES, len(chunks)):
+        own_chunk(chunks[n])
         if tree:
-            pass_on(d - 1)
-        if tree and d >= 2:
-            pass_diagonal(d - 2)
+            pass_on(chunks[n - 1])
+            pass_diagonal(chunks[n - 2])
     for copy in small3:
         copy.wait_recv()
 
-    def scored(r, best):
+    def scored(r, h, best):
+        first = h * part
+        if r:
+            for d in range(groups):
+                for side in (0, 1) if tree and r >= 6 else (None,):
+                    arrive(r, (h, d), side)
         scores = lax.dot_general(
-            held[r], held[0], (((1,), (1,)), ((), ())), preferred_element_type=jnp.float32
-        )
-        key = column(keys[r])
+            held[r, first : first + part],
+            held[0],
+            (((1,), (1,)), ((), ())),
+            preferred_element_type=jnp.float32,
+        )
+        key = column(keys[r][:, first : first + part])
         allowed = (key >= query_low) & (key < query_key)
         return jnp.maximum(
             best, jnp.max(jnp.where(allowed, scores, -1.0), axis=0, keepdims=True)
         )
 
     best = jnp.full((1, rows), -1.0, jnp.float32)
+    for h in range(HALVES):
+        best = scored(0, h, best)
     if tree:
-        pass_on(groups - 1)
-        pass_diagonal(groups - 2)
-        best = scored(0, best)
-        for r in (2, 4):
-            best = scored(r, best)
-        pass_diagonal(groups - 1)
-        for r in (1, 3, 5):
-            for d in range(groups):
-                arrive(r, d)
-            best = scored(r, best)
-        best = scored(6, best)
-        for d in range(groups):
-            for part in (0, 1):
-                arrive(7, d, part)
-        best = scored(7, best)
+        pass_on(chunks[-1])
+        pass_diagonal(chunks[-2])
+        for r in (2, 4, 1, 3, 5):
+            best = scored(r, 0, best)
+        pass_diagonal(chunks[-1])
+        for r, h in ((6, 0), (7, 0), (2, 1), (4, 1), (1, 1), (6, 1), (3, 1), (5, 1), (7, 1)):
+            best = scored(r, h, best)
     else:
-        best = scored(0, best)
         for r in range(1, members):
-            for d in range(groups):
-                arrive(r, d)
-            best = scored(r, best)
+            for h in range(HALVES):
+                best = scored(r, h, best)
 
     score2[...] = best
     home2 = [
@@ -293,7 +316,7 @@
         copy.wait_recv()
     merged = best
     for d in range(1, groups):
-        merged = jnp.where(lax.div(lane, share) == d, back2[d], merged)
+        merged = jnp.where(lax.div(lax.rem(lane, part), share) == d, back2[d], merged)
     best = jnp.max(jnp.where(sub == slot2, column(merged), -2.0), axis=0, keepdims=True)
     score1[...] = best
     home1 = [
@@ -304,12 +327,12 @@
         copy.wait_recv()
     merged = best
     for r in range(1, members):
-        merged = jnp.where(lax.div(lane, deal) == r, back1[r], merged)
+        merged = jnp.where(lax.div(lax.rem(lane, part), deal) == r, back1[r], merged)
     out_ref[...] = jnp.max(jnp.where(sub == slot1, column(merged), -2.0), axis=0, keepdims=True)
 
     for copy in [
         *small,
-        *copies1,
+        *copies1.values(),
         *small2,
         *copies2.values(),
         *small3,
@@ -348,12 +371,12 @@
             pltpu.VMEM((1, rows), jnp.float32),
             pltpu.VMEM((members, 1, rows), jnp.float32),
             pltpu.SemaphoreType.DMA((3,)),
-            pltpu.SemaphoreType.DMA((members,)),
-            pltpu.SemaphoreType.DMA((members,)),
-            pltpu.SemaphoreType.DMA((groups,)),
-            pltpu.SemaphoreType.DMA((groups,)),
-            pltpu.SemaphoreType.DMA((members, groups, 2)),
-            pltpu.SemaphoreType.DMA((members, groups, 2)),
+            pltpu.SemaphoreType.DMA((HALVES, members)),
+            pltpu.SemaphoreType.DMA((HALVES, members)),
+            pltpu.SemaphoreType.DMA((HALVES, groups)),
+            pltpu.SemaphoreType.DMA((HALVES, groups)),
+            pltpu.SemaphoreType.DMA((members, HALVES * groups, 2)),
+            pltpu.SemaphoreType.DMA((members, HALVES * groups, 2)),
             pltpu.SemaphoreType.DMA((members,)),
             pltpu.SemaphoreType.DMA((members,)),
             pltpu.SemaphoreType.DMA((groups,)),

time: 65 us -> 61 us (0.938)
  Pallas kernels: 61.7 us -> 57.7 us
    pallas_call x1, Pallas kernels: 61.7 us -> 57.7 us  [body(): pl.pallas_call(functools.partial(kernel, groups, members), out_shape=jax....]
where the time goes in v3:
time: 61 us; the launch traced here: 60.8 us
  Pallas kernels  57.7 us (95%)
  local copies, waits for them, and re-layouts  3.08 us (5%)
    pallas_call x1, Pallas kernels, body(): pl.pallas_call(functools.partial(kernel, groups, members), out_shape=jax....  57.7 us
    unnamed x7, local copies, waits for them, and re-layouts  3.08 us

profile of v3, /device:TPU:0, one launch (start us, length us, event | category | flops | bytes accessed | tf_op | source)
XLA Modules:
  0.0 60.8 jit_solution(9710699888201187700)
XLA Ops:
  0.0 0.0 copy-start.1
  0.0 0.7 %copy-done.1 = s32[512]{0:T(512)S(1)} copy-done((s32[512]{0:T(512)S(1)}, s32[512]{0:T(512)}, u32[]{:S(2)}) %copy-start.1) | copy-done | bytes 2072
  0.7 0.0 copy-start
  0.7 1.1 %copy-done = bf16[512,768]{1,0:T(8,128)(2,1)S(1)} copy-done((bf16[512,768]{1,0:T(8,128)(2,1)S(1)}, bf16[512,768]{1,0:T(8,128)(2,1)}, u32[]{:S(2)}) %copy-start) | copy-done | bytes 786456
  1.8 0.0 copy-start.2
  1.8 0.7 %copy-done.2 = s32[512]{0:T(512)S(1)} copy-done((s32[512]{0:T(512)S(1)}, s32[512]{0:T(512)}, u32[]{:S(2)}) %copy-start.2) | copy-done | bytes 2072
  2.5 57.7 %shard_map.37 = f32[1,512]{1,0:T(1,128)S(1)} custom-call(bf16[512,768]{1,0:T(8,128)(2,1)S(1)} %copy-done, s32[1,512]{1,0:T(1,128)S(1)} %bitcast.4, s32[1,512]{1,0:T(1,128)S(1)} %bitcast.5), custom_call_target="tpu_custom_call" | custom-call | tf_op jit(solution)/shard_map/pallas_call | solution.py:350
  60.3 0.6 copy.5
Async XLA Ops:
  0.0 0.7 %copy-start.1 = (s32[512]{0:T(512)S(1)}, s32[512]{0:T(512)}, u32[]{:S(2)}) copy-start(s32[512]{0:T(512)} %param.4) | copy-start | bytes 6148
  0.7 1.1 %copy-start = (bf16[512,768]{1,0:T(8,128)(2,1)S(1)}, bf16[512,768]{1,0:T(8,128)(2,1)}, u32[]{:S(2)}) copy-start(bf16[512,768]{1,0:T(8,128)(2,1)} %emb_ref.1) | copy-start | bytes 2359300
  1.8 0.7 %copy-start.2 = (s32[512]{0:T(512)S(1)}, s32[512]{0:T(512)}, u32[]{:S(2)}) copy-start(s32[512]{0:T(512)} %param.5) | copy-start | bytes 6148

commit v4 on v3

--- a/solution.py
+++ b/solution.py
@@ -230,7 +230,8 @@
     def own_chunk(chunk):
         if chunk[1]:
             copies2[chunk].wait_recv()
-        for r in (2, 4, 1) if tree else range(1, members):
+        near = (2, 4, 1) if sum(chunk) % 2 == 0 else (4, 2, 1)
+        for r in near if tree else range(1, members):
             forward(0, r, chunk, None, r)
 
     def pass_on(chunk):

time: 61 us -> 61 us (level)
  no operation moved by 1% of the time
where the time goes in v4:
time: 61 us; the launch traced here: 60.8 us
  Pallas kernels  57.7 us (95%)
  local copies, waits for them, and re-layouts  3.08 us (5%)
    pallas_call x1, Pallas kernels, body(): pl.pallas_call(functools.partial(kernel, groups, members), out_shape=jax....  57.7 us
    unnamed x7, local copies, waits for them, and re-layouts  3.08 us

profile of v4, /device:TPU:0, one launch (start us, length us, event | category | flops | bytes accessed | tf_op | source)
XLA Modules:
  0.0 60.8 jit_solution(13356167426366201244)
XLA Ops:
  0.0 0.0 copy-start.1
  0.0 0.7 %copy-done.1 = s32[512]{0:T(512)S(1)} copy-done((s32[512]{0:T(512)S(1)}, s32[512]{0:T(512)}, u32[]{:S(2)}) %copy-start.1) | copy-done | bytes 2072
  0.7 0.0 copy-start
  0.7 1.1 %copy-done = bf16[512,768]{1,0:T(8,128)(2,1)S(1)} copy-done((bf16[512,768]{1,0:T(8,128)(2,1)S(1)}, bf16[512,768]{1,0:T(8,128)(2,1)}, u32[]{:S(2)}) %copy-start) | copy-done | bytes 786456
  1.8 0.0 copy-start.2
  1.8 0.7 %copy-done.2 = s32[512]{0:T(512)S(1)} copy-done((s32[512]{0:T(512)S(1)}, s32[512]{0:T(512)}, u32[]{:S(2)}) %copy-start.2) | copy-done | bytes 2072
  2.5 57.7 %shard_map.37 = f32[1,512]{1,0:T(1,128)S(1)} custom-call(bf16[512,768]{1,0:T(8,128)(2,1)S(1)} %copy-done, s32[1,512]{1,0:T(1,128)S(1)} %bitcast.4, s32[1,512]{1,0:T(1,128)S(1)} %bitcast.5), custom_call_target="tpu_custom_call" | custom-call | tf_op jit(solution)/shard_map/pallas_call | solution.py:351
  60.2 0.6 copy.5
Async XLA Ops:
  0.0 0.7 %copy-start.1 = (s32[512]{0:T(512)S(1)}, s32[512]{0:T(512)}, u32[]{:S(2)}) copy-start(s32[512]{0:T(512)} %param.4) | copy-start | bytes 6148
  0.7 1.1 %copy-start = (bf16[512,768]{1,0:T(8,128)(2,1)S(1)}, bf16[512,768]{1,0:T(8,128)(2,1)}, u32[]{:S(2)}) copy-start(bf16[512,768]{1,0:T(8,128)(2,1)} %emb_ref.1) | copy-start | bytes 2359300
  1.8 0.7 %copy-start.2 = (s32[512]{0:T(512)S(1)}, s32[512]{0:T(512)}, u32[]{:S(2)}) copy-start(s32[512]{0:T(512)} %param.5) | copy-start | bytes 6148
